TPU v7x, 256 devices: a whole 4x4x8 slice. The times are simulated.
256 devices in a mesh: space: 16 (over x, y), chan: 4 (over z_lo, core), filt: 4 (over z_hi).
Axes of the slice: x: 4, y: 4, z: 8 (z_hi: 4, z_lo: 2; z = z_hi * 2 + z_lo), core: 2. Of those that a mesh axis runs over, the one named last changes fastest.
Arguments:
- field: float32 [256, 4, 128, 256], P('chan', 'filt', 'space'), may hold values from -6 to 6
- weight: float32 [3, 3, 3, 256, 256], P(None, None, None, 'chan'), may hold values from -0.078125 to 0.078125
- bias: float32 [256], P('filt'), may hold values from -0.5 to 0.5
Outputs:
- output: float32 [256, 4, 128, 256], P('filt', 'chan', 'space')
All inputs are finite; a program needn't handle non-finite values.
Results may differ from a plain program's by a relative error of at most 0.000073.
Values sent between devices are 32-bit elements; how exact they have to be, the bound alone decides.
A program may use at most 64 MiB of HBM per device.

v0:
```python
import jax
import jax.numpy as jnp
from jax import lax
from jax.sharding import PartitionSpec as P


def extended(block, sides, width):
    for axis, dim in sides:
        count = lax.axis_size(axis)
        forward = [(i, i + 1) for i in range(count - 1)]
        backward = [(target, source) for source, target in forward]
        low = lax.ppermute(
            lax.slice_in_dim(block, block.shape[dim] - width, None, axis=dim), axis, forward
        )
        high = lax.ppermute(lax.slice_in_dim(block, 0, width, axis=dim), axis, backward)
        block = jnp.concatenate([low, block, high], axis=dim)
    return block


def convolve(padded, kernel):
    oriented = jnp.transpose(kernel, (4, 3, 0, 1, 2))
    result = lax.conv_general_dilated(
        padded[None],
        oriented,
        (1, 1, 1),
        "VALID",
        dimension_numbers=("NCDHW", "OIDHW", "NCDHW"),
        precision=lax.Precision.HIGHEST,
        preferred_element_type=jnp.float32,
    )
    return result[0]


def per_device(field, weight, bias):
    filters_own = bias.shape[0]
    kernel = lax.dynamic_slice_in_dim(weight, lax.axis_index("filt") * filters_own, filters_own, 4)
    gathered = lax.all_gather(field, "filt", axis=1, tiled=True)
    padded = extended(gathered, (("space", 2),), 1)
    count_z = padded.shape[1]
    padded = jnp.pad(padded, ((0, 0), (1, 1), (0, 0), (1, 1)))
    running = convolve(padded, kernel)
    planes_own = count_z // lax.axis_size("chan")
    summed = lax.psum(running, "chan")
    summed = lax.dynamic_slice_in_dim(summed, lax.axis_index("chan") * planes_own, planes_own, 1)
    return jax.nn.silu(summed + bias[:, None, None, None])


def solution(mesh):
    placed = (P("chan", "filt", "space", None), P(None, None, None, "chan", None), P("filt"))
    return jax.shard_map(
        per_device,
        mesh=mesh,
        in_specs=placed,
        out_specs=P("filt", "chan", "space", None),
        check_vma=False,
    )
```

profile of v0, /device:TPU:1, one launch (start us, length us, event | category | flops | bytes accessed | tf_op | source)
XLA Modules:
  0.0 254.7 jit_solution(12627410079857861010)
XLA Ops:
  6.5 0.0 copy-start
  6.5 0.0 all-gather.2.cloned.1.call-start
  6.5 0.7 all-gather.2.cloned.1.call-update
  7.3 0.0 all-reduce.3.cloned.1.call-start
  7.3 54.5 %all-gather.2.cloned.1.call-done = f32[64,4,8,256]{3,2,0,1:T(8,128)} async-done(((f32[64,1,8,256]{3,2,0,1:T(8,128)}), f32[64,4,8,256]{3,2,0,1:T(8,128)}) %all-gather.2.cloned.1.call-update) | async-done | bytes 2097168 | tf_op jit(solution)/shard_map/all_gather | solution.py:37
  61.8 2.6 %fusion.18 = (f32[64,4,1,256]{3,2,0,1:T(1,128)S(1)}, f32[64,4,1,256]{3,2,0,1:T(1,128)S(1)}) fusion(f32[64,4,8,256]{3,2,0,1:T(8,128)} %all-gather.2.cloned.1.call-done), kind=kLoop, calls=%fused_computation.25 | loop fusion | bytes 1048576 | tf_op jit(solution)/shard_map/slice | solution.py:13
  64.4 1.3 collective-permute-start.1
  65.7 6.5 %collective-permute-start = (f32[64,4,1,256]{3,0,2,1:T(8,128)S(1)}, f32[64,4,1,256]{3,0,2,1:T(8,128)}, u32[]{:S(2)}, u32[]{:S(2)}) collective-permute-start(f32[64,4,1,256]{3,0,2,1:T(8,128)S(1)} %copy.26), channel_id=1, source_target_pairs={{0,16},{16,32},{32,48},{48,64},{64,80},{80,96},{96,112},{112,128},... | collective-permute-start | bytes 786440 | tf_op jit(solution)/shard_map/ppermute | solution.py:12
  72.2 0.0 copy-done
  72.2 0.3 fusion.25
  72.5 2.0 collective-permute-done.1
  74.5 0.3 copy.29
  74.8 0.7 collective-permute-done
  75.4 1.2 copy.28
  76.6 7.5 %fusion = f32[64,6,10,1,258]{4,2,0,1,3:T(8,128)} fusion(f32[64,4,1,256]{3,2,0,1:T(1,128)S(1)} %copy.29, f32[64,4,8,256]{3,2,0,1:T(8,128)} %all-gather.2.cloned.1.call-done, f32[64,4,1,256]{3,2,0,1:T(1,128)S(1)} %copy.28), kind=kLoop, calls=%fused_computation.5 | loop fusion | flops 14860800 | bytes 6584320 | tf_op jit(solution)/shard_map/broadcast_in_dim | solution.py:23
  84.1 24.1 %copy.36 = f32[64,6,10,1,258]{0,3,4,2,1:T(1,128)} copy(f32[64,6,10,1,258]{4,2,0,1,3:T(8,128)} %fusion) | data formatting | bytes 7925760
  108.2 7.1 %pad.5.clone = f32[64,6,10,1,264]{0,3,4,2,1:T(1,128)S(1)} pad(f32[64,6,10,1,258]{0,3,4,2,1:T(1,128)} %copy.36, f32[]{:T(128)} %constant.5.clone.1), padding=0_0x0_0x0_0x0_0x0_6 | pad | bytes 8017924 | tf_op jit(solution)/shard_map/broadcast_in_dim | solution.py:23
  115.4 0.0 copy-start.2
  115.4 0.5 copy.32
  115.9 0.1 copy-done.2
  116.0 55.3 %broadcast_select_fusion = f32[4,8,8,33,64]{4,2,3,1,0:T(8,128)S(1)} fusion(pred[8,33]{0,1:T(8,128)(4,1)S(1)} %copy-done.2, f32[64,6,10,1,7,2]{0,4,5,2,1,3:T(8,128)S(1)} %slice.12, f32[64,6,10,1,8,33]{0,4,5,2,1,3:T(8,128)S(1)} %copy.32, f32[3,3,3,64,64]{4,3,2,1,0:T(8,128)S(1)} %fusion.25), kind=kOutput, calls=%fused_computation.18 | convolution fusion | flops 11215140864 | bytes 6875400 | tf_op jit(solution)/shard_map/conv_general_dilated | solution.py:22
  171.3 0.8 copy.33
  172.1 0.0 copy-start.1
  172.1 2.2 slice.13
  174.4 4.5 %copy.35 = f32[4,8,1,256,64]{3,1,0,4,2:T(8,128)} copy(f32[4,8,1,256,64]{4,1,3,0,2:T(8,128)} %slice.13) | data formatting | bytes 4194304
  178.9 0.0 all-reduce.3.cloned.1.call-update
  178.9 66.9 %all-reduce.3.cloned.1.call-done = f32[64,4,8,256]{3,2,1,0:T(8,128)} async-done(((f32[64,4,8,256]{3,2,1,0:T(8,128)}), f32[64,4,8,256]{3,2,1,0:T(8,128)}) %all-reduce.3.cloned.1.call-update) | async-done | bytes 2097168 | tf_op jit(solution)/shard_map/psum | solution.py:43
  245.8 0.0 copy-done.1
  245.8 2.0 divide_multiply_fusion
  (3 shorter events, 0.1 us)
Async XLA Ops:
  6.5 65.6 %copy-start = (f32[3,3,3,64,256]{4,3,2,1,0:T(8,128)S(1)}, f32[3,3,3,64,256]{4,3,2,1,0:T(8,128)}, u32[]{:S(2)}) copy-start(f32[3,3,3,64,256]{4,3,2,1,0:T(8,128)} %param.4) | copy-start | bytes 5308420
  6.5 55.2 %all-gather.2.cloned.1.call-start = ((), (), s32[]{:S(2)}) async-start(), calls=%async_computation | async-start | bytes 2621440 | tf_op jit(solution)/shard_map/all_gather | solution.py:37
  7.3 238.5 %all-reduce.3.cloned.1.call-start = ((), (), s32[]{:S(2)}) async-start(), calls=%async_computation.1 | async-start | bytes 4194304 | tf_op jit(solution)/shard_map/psum | solution.py:43
  64.4 10.1 %collective-permute-start.1 = (f32[64,4,1,256]{3,0,2,1:T(8,128)S(1)}, f32[64,4,1,256]{3,0,2,1:T(8,128)S(1)}, u32[]{:S(2)}, u32[]{:S(2)}) collective-permute-start(f32[64,4,1,256]{3,0,2,1:T(8,128)S(1)} %copy.27), channel_id=1, source_target_pairs={{16,0},{32,16},{48,32},{64,48},{80,64},{96,80},{112,96},{128,112},... | collective-permute-start | bytes 786440 | tf_op jit(solution)/shard_map/ppermute | solution.py:15
  65.7 9.7 %collective-permute-start = (f32[64,4,1,256]{3,0,2,1:T(8,128)S(1)}, f32[64,4,1,256]{3,0,2,1:T(8,128)}, u32[]{:S(2)}, u32[]{:S(2)}) collective-permute-start(f32[64,4,1,256]{3,0,2,1:T(8,128)S(1)} %copy.26), channel_id=1, source_target_pairs={{0,16},{16,32},{32,48},{48,64},{64,80},{80,96},{96,112},{112,128},... | collective-permute-start | bytes 786440 | tf_op jit(solution)/shard_map/ppermute | solution.py:12
  115.4 0.7 copy-start.2
  172.1 73.7 %copy-start.1 = (f32[64]{0:T(128)S(1)}, f32[64]{0:T(128)}, u32[]{:S(2)}) copy-start(f32[64]{0:T(128)} %param.5) | copy-start | bytes 772
Sparse Core Ops, SparseCore 0:
  9.2 52.5 all-gather.1
  179.0 66.7 all-reduce.2
where the time goes:
time: 256 us; the launch traced here: 255 us
  waiting for transfers between devices  125 us (49%)
  matrix products  55.3 us (22%)
  local copies, waits for them, and re-layouts  43.8 us (17%)
  between operations  13.5 us (5%)
  other arithmetic  9.56 us (4%)
  starting transfers between devices  7.78 us (3%)
    psum x1, waiting for transfers between devices, per_device(): summed = lax.psum(running, 'chan')  66.9 us
    conv_general_dilated x1, matrix products, convolve(): lax.conv_general_dilated(padded[None], oriented, (1, 1, 1), 'VALID', dime...  55.3 us
    all_gather x1, waiting for transfers between devices, per_device(): gathered = lax.all_gather(field, 'filt', axis=1, tiled=True)  54.5 us
    unnamed x8, local copies, waits for them, and re-layouts  28.7 us
    broadcast_in_dim x1, other arithmetic, convolve(): padded[None]  7.51 us
    broadcast_in_dim x1, local copies, waits for them, and re-layouts, convolve(): padded[None]  7.12 us
    ppermute x1, starting transfers between devices, extended(): lax.ppermute(lax.slice_in_dim(block, block.shape[dim] - width, None, axis...  6.45 us
  transfers between devices with their start and end apart: 4, of which 4 were waited for; matrix products, arithmetic and copies ran while one was open for 0% of the time, Pallas kernels for 0%

commit v1 on v0

v1 whole, which is shorter than its diff:
```python
import jax
import jax.numpy as jnp
from jax import lax
from jax.experimental import pallas as pl
from jax.experimental.pallas import tpu as pltpu
from jax.sharding import PartitionSpec as P

MESH = pl.DeviceIdType.MESH
CHUNKS = ((0, 7, 0), (7, 7, 1), (14, 7, 0), (21, 6, 1))
F32, BF16 = jnp.float32, jnp.bfloat16


def split(value):
    high = value.astype(BF16)
    return high, (value - high.astype(F32)).astype(BF16)


def kernel(
    f_ref, w_ref, b_ref, o_ref,
    turned, out_in, got_in, cells, taps, weight_own, weight_other, wcat, total, sibling, out_back, got_back,
    own_sem, swap_ss, swap_rs, a_ss, a_rs, b_ss, b_rs, in_ss, in_rs, halo_ss, halo_rs, sib_ss, sib_rs, back_ss, back_rs,
):
    s, c, h = lax.axis_index("space"), lax.axis_index("chan"), lax.axis_index("filt")
    xx, yy = s // 4, s % 4
    lo, core = c // 2, c % 2
    z = 2 * h + lo

    def column(other_z, other_core):
        return (s, (other_z % 2) * 2 + other_core, other_z // 2)

    def plane(other_x, other_y):
        return (other_x * 4 + other_y, c, h)

    own = pltpu.make_async_copy(w_ref, weight_own, own_sem)
    own.start()

    barrier = pltpu.get_barrier_semaphore()
    greet = []
    for dz in range(8):
        for dk in range(2):
            if dz or dk:
                greet.append(column((z + dz) % 8, (core + dk) % 2))
    for d in range(1, 4):
        greet.append(plane((xx + d) % 4, yy))
        greet.append(plane(xx, (yy + d) % 4))
    greet.append(((s + 1) % 16, c, h))
    greet.append(((s + 15) % 16, c, h))
    for device in greet:
        pl.semaphore_signal(barrier, 1, device_id=device, device_id_type=MESH)
    pl.semaphore_wait(barrier, len(greet))

    def piece(ref, first, count, turn):
        u, v = (yy, xx) if turn else (xx, yy)
        rows = pl.multiple_of(16 * u + 8 * (v // 2), 8)
        lanes = pl.multiple_of(128 * (v % 2), 128)
        return ref.at[pl.ds(first, count), pl.ds(rows, 8), pl.ds(lanes, 128)]

    def band(ref, first, count, turn):
        u = yy if turn else xx
        return ref.at[pl.ds(first, count), pl.ds(pl.multiple_of(16 * u, 16), 16), :]

    swaps = []
    for q, (first, count, turn) in enumerate(CHUNKS):
        target = column((z + (7 if turn else 1)) % 8, core)
        swaps.append(
            pltpu.make_async_remote_copy(
                piece(w_ref, first, count, turn), piece(weight_other, first, count, turn),
                swap_ss.at[q], swap_rs.at[q], device_id=target, device_id_type=MESH,
            )
        )
        swaps[-1].start()

    lane = lax.broadcasted_iota(jnp.int32, (1, 128), 1)
    left = lane < 64
    for x in range(8):
        rows = f_ref[:, x, :]
        turned[x, 8:264, :] = jnp.concatenate([rows, rows], axis=0).T
        turned[x, 0:8, :] = jnp.zeros((8, 128), F32)
        turned[x, 264:272, :] = jnp.zeros((8, 128), F32)
    for t in range(8):
        base = 8 + 32 * t
        for x in range(8):
            out_in[t, 16 * x : 16 * x + 16, :] = jnp.where(
                left, turned[x, base : base + 16, :], turned[x, base + 16 : base + 32, :]
            )
        low_side = turned[:, base - 8 : base, :][:, 7, :]
        high_side = turned[:, base + 32 : base + 40, :][:, 0, :]
        out_in[t, 128:136, :] = jnp.where(left, low_side, high_side)
    ins = []
    for n, dz in enumerate((4, 3, 5, 2, 6, 1, 7)):
        target = (z + dz) % 8
        ins.append(
            pltpu.make_async_remote_copy(
                out_in.at[target], got_in.at[z], in_ss.at[n], in_rs.at[z],
                device_id=column(target, core), device_id_type=MESH,
            )
        )
        ins[-1].start()
    got_in[z] = out_in[z]

    @pl.when(s == 0)
    def _():
        cells[:, 0, :, :] = jnp.zeros((4, 48, 128), F32)

    @pl.when(s == 15)
    def _():
        cells[:, 9, :, :] = jnp.zeros((4, 48, 128), F32)

    spread_a, spread_b = [], []
    for q, (first, count, turn) in enumerate(CHUNKS):
        swaps[q].wait_recv()
        for d in range(1, 4):
            target = plane((xx + d) % 4, yy) if turn else plane(xx, (yy + d) % 4)
            block = piece(weight_other, first, count, turn)
            copy = pltpu.make_async_remote_copy(
                block, block, a_ss.at[q, d - 1], a_rs.at[q, d - 1], device_id=target, device_id_type=MESH
            )
            copy.start()
            spread_a.append(copy)
    for q, (first, count, turn) in enumerate(CHUNKS):
        for d in range(3):
            spread_a[3 * q + d].wait_recv()
        for d in range(1, 4):
            target = plane(xx, (yy + d) % 4) if turn else plane((xx + d) % 4, yy)
            block = band(weight_other, first, count, turn)
            copy = pltpu.make_async_remote_copy(
                block, block, b_ss.at[q, d - 1], b_rs.at[q, d - 1], device_id=target, device_id_type=MESH
            )
            copy.start()
            spread_b.append(copy)

    def convert(source, half, first, count):
        @pl.loop(first, first + count)
        def _(tap):
            ab, y = tap // 3, tap % 3
            high, low = split(source[tap])
            for place, value in ((256 * y, high), (256 * y + 128, high), (768 + 128 * y, low)):
                wcat[ab, pl.ds(pl.multiple_of(place + 64 * half, 64), 64), :] = value

    own.wait()
    convert(weight_own, lo, 0, 27)

    for n, dz in enumerate((7, 1, 6, 2, 5, 3, 4)):
        source = (z + dz) % 8
        pltpu.make_async_remote_copy(
            out_in.at[z], got_in.at[source], in_ss.at[n], in_rs.at[source],
            device_id=column(source, core), device_id_type=MESH,
        ).wait_recv()

    @pl.loop(0, 4)
    def _(p):
        for x in range(8):
            first = got_in[2 * p, 16 * x : 16 * x + 16, :]
            second = got_in[2 * p + 1, 16 * x : 16 * x + 16, :]
            cells[p, 1 + x, 8:24, :] = jnp.where(left, first, pltpu.roll(second, 64, 1))
            cells[p, 1 + x, 24:40, :] = jnp.where(left, pltpu.roll(first, 64, 1), second)
        first = got_in[2 * p, 128:136, :]
        second = got_in[2 * p + 1, 128:136, :]
        low_side = jnp.where(left, first, pltpu.roll(second, 64, 1))
        high_side = jnp.where(left, pltpu.roll(first, 64, 1), second)
        for x in range(8):
            cells[p, 1 + x, 7:8, :] = low_side[x : x + 1]
            cells[p, 1 + x, 40:41, :] = high_side[x : x + 1]

    up = pltpu.make_async_remote_copy(
        cells.at[:, 8], cells.at[:, 0], halo_ss.at[0], halo_rs.at[0],
        device_id=((s + 1) % 16, c, h), device_id_type=MESH,
    )
    down = pltpu.make_async_remote_copy(
        cells.at[:, 1], cells.at[:, 9], halo_ss.at[1], halo_rs.at[1],
        device_id=((s + 15) % 16, c, h), device_id_type=MESH,
    )

    @pl.when(s < 15)
    def _():
        up.start()

    @pl.when(s > 0)
    def _():
        down.start()

    def spread(x):
        @pl.loop(0, 4)
        def _(p):
            for y in range(3):
                high, low = split(cells[p, x, 7 + y : 39 + y, :])
                taps[p, x, :, 256 * y : 256 * y + 128] = high
                taps[p, x, :, 256 * y + 128 : 256 * y + 256] = low
                taps[p, x, :, 768 + 128 * y : 896 + 128 * y] = high

    @pl.loop(1, 9)
    def _(x):
        spread(x)

    @pl.when(s > 0)
    def _():
        up.wait_recv()

    @pl.when(s < 15)
    def _():
        down.wait_recv()

    spread(0)
    spread(9)

    for copy in spread_b:
        copy.wait_recv()
    convert(weight_other, 1 - lo, 0, 27)

    def group(g, slot):
        edge, inner, far = 3 * g, 1 + g, 2 - g
        onward = 2 - 2 * g

        def left_side(p, b):
            return taps[p, pl.ds(b, 8)].reshape(256, 1152)

        for b in range(3):
            first, second, third = left_side(edge, b), left_side(inner, b), left_side(far, b)
            same = jnp.dot(
                jnp.concatenate([first, second], axis=0), wcat[3 + b], preferred_element_type=F32
            )
            if b == 0:
                total[slot] = same
            else:
                total[slot] += same
            total[slot] += jnp.dot(
                jnp.concatenate([second, third], axis=0), wcat[3 * onward + b], preferred_element_type=F32
            )
            total[slot, 256:512, :] += jnp.dot(first, wcat[3 * (2 - onward) + b], preferred_element_type=F32)

    group(1 - core, 0)
    exchange = pltpu.make_async_remote_copy(
        total.at[0], sibling, sib_ss, sib_rs, device_id=column(z, 1 - core), device_id_type=MESH
    )
    exchange.start()
    group(core, 1)
    exchange.wait_recv()

    for n in range(2):
        p = (3 * core, 1 + core)[n]
        for pair in range(2):
            rows, lanes = slice(256 * n, 256 * n + 256), slice(128 * pair, 128 * pair + 128)
            value = (total[1, rows, lanes] + sibling[rows, lanes]).reshape(8, 32, 128)
            low_part = value[:, :16, :].reshape(128, 128)
            high_part = value[:, 16:, :].reshape(128, 128)
            out_back[4 * n + 2 * pair] = jnp.where(left, low_part, pltpu.roll(high_part, 64, 1))
            out_back[4 * n + 2 * pair + 1] = jnp.where(left, pltpu.roll(low_part, 64, 1), high_part)
            for f in (2 * pair, 2 * pair + 1):
                here = jnp.logical_and(p == c, f == h)
                block = 4 * n + f

                @pl.when(here)
                def _():
                    pltpu.make_async_copy(out_back.at[block], got_back.at[z], back_rs.at[z]).start()

                @pl.when(jnp.logical_not(here))
                def _():
                    pltpu.make_async_remote_copy(
                        out_back.at[block], got_back.at[z], back_ss.at[block], back_rs.at[z],
                        device_id=(s, p, f), device_id_type=MESH,
                    ).start()

    for source in range(8):
        pltpu.make_async_copy(got_back.at[source], got_back.at[source], back_rs.at[source]).wait()

    bias = b_ref[...].reshape(1, 64)
    bias = jnp.concatenate([bias, bias], axis=1)
    for x in range(8):
        value = got_back[:, 16 * x : 16 * x + 16, :] + bias.reshape(1, 1, 128)
        value = value / (1.0 + jnp.exp(-value))
        value = value.reshape(128, 128)
        other = pltpu.roll(value, 64, 1)
        rows = jnp.stack([value.reshape(8, 16, 128), other.reshape(8, 16, 128)], axis=1).reshape(256, 128)
        o_ref[:, x, :] = rows.T[:64, :]

    for copy in swaps + spread_a + spread_b + ins + [exchange]:
        copy.wait_send()

    @pl.when(s < 15)
    def _():
        up.wait_send()

    @pl.when(s > 0)
    def _():
        down.wait_send()

    for n in range(2):
        p = (3 * core, 1 + core)[n]
        for f in range(4):
            block = 4 * n + f

            @pl.when(jnp.logical_not(jnp.logical_and(p == c, f == h)))
            def _():
                pltpu.make_async_remote_copy(
                    out_back.at[block], got_back.at[z], back_ss.at[block], back_rs.at[z],
                    device_id=(s, p, f), device_id_type=MESH,
                ).wait_send()


def per_device(field, weight, bias):
    dma, chunks = pltpu.SemaphoreType.DMA, len(CHUNKS)
    result = pl.pallas_call(
        kernel,
        out_shape=jax.ShapeDtypeStruct((64, 8, 256), F32),
        in_specs=[
            pl.BlockSpec(memory_space=pltpu.VMEM),
            pl.BlockSpec(memory_space=pl.ANY),
            pl.BlockSpec(memory_space=pltpu.VMEM),
        ],
        out_specs=pl.BlockSpec(memory_space=pltpu.VMEM),
        scratch_shapes=[
            pltpu.VMEM((8, 272, 128), F32),
            pltpu.VMEM((8, 136, 128), F32),
            pltpu.VMEM((8, 136, 128), F32),
            pltpu.VMEM((4, 10, 48, 128), F32),
            pltpu.VMEM((4, 10, 32, 1152), BF16),
            pltpu.VMEM((27, 64, 256), F32),
            pltpu.VMEM((27, 64, 256), F32),
            pltpu.VMEM((9, 1152, 256), BF16),
            pltpu.VMEM((2, 512, 256), F32),
            pltpu.VMEM((512, 256), F32),
            pltpu.VMEM((8, 128, 128), F32),
            pltpu.VMEM((8, 128, 128), F32),
            dma,
            dma((chunks,)),
            dma((chunks,)),
            dma((chunks, 3)),
            dma((chunks, 3)),
            dma((chunks, 3)),
            dma((chunks, 3)),
            dma((7,)),
            dma((8,)),
            dma((2,)),
            dma((2,)),
            dma,
            dma,
            dma((8,)),
            dma((8,)),
        ],
        compiler_params=pltpu.CompilerParams(
            collective_id=0, has_side_effects=True, vmem_limit_bytes=48 * 2**20
        ),
        cost_estimate=pl.CostEstimate(flops=4 * 10**9, bytes_accessed=4 * 10**6, transcendentals=131072),
        name="convolution",
    )(field.reshape(64, 8, 256), weight.reshape(27, 64, 256), bias)
    return result.reshape(64, 1, 8, 256)


def solution(mesh):
    placed = (P("chan", "filt", "space", None), P(None, None, None, "chan", None), P("filt"))
    return jax.shard_map(
        per_device,
        mesh=mesh,
        in_specs=placed,
        out_specs=P("filt", "chan", "space", None),
        check_vma=False,
    )
```

time: 256 us -> 59.4 us (0.23)
  waiting for transfers between devices: 125 us -> 0 us
  matrix products: 55.3 us -> 0 us
  Pallas kernels: 0 us -> 55.2 us
  local copies, waits for them, and re-layouts: 43.8 us -> 3.97 us
  between operations: 13.5 us -> 0.01 us
  other arithmetic: 9.56 us -> 0 us
  starting transfers between devices: 7.78 us -> 0 us
    psum x1 -> x0, waiting for transfers between devices: 66.9 us -> none  [per_device(): summed = lax.psum(running, 'chan')]
    conv_general_dilated x1 -> x0, matrix products: 55.3 us -> none  [convolve(): lax.conv_general_dilated(padded[None], oriented, (1, 1, 1), 'VALID', dime...]
    pallas_call x0 -> x1, Pallas kernels: none -> 55.2 us  [per_device(): pl.pallas_call(kernel, out_shape=jax.ShapeDtypeStruct((64, 8, 256), F32),...]
    all_gather x1 -> x0, waiting for transfers between devices: 54.5 us -> none  [per_device(): gathered = lax.all_gather(field, 'filt', axis=1, tiled=True)]
    unnamed x8 -> x7, local copies, waits for them, and re-layouts: 28.7 us -> 3.97 us
    ppermute x2 -> x0, starting transfers between devices: 7.74 us -> none  [the longest x1 6.45 us: extended(): lax.ppermute(lax.slice_in_dim(block, block.shape[dim] - width, None, axis...]
    broadcast_in_dim x1 -> x0, other arithmetic: 7.51 us -> none  [convolve(): padded[None]]
    broadcast_in_dim x1 -> x0, local copies, waits for them, and re-layouts: 7.12 us -> none  [convolve(): padded[None]]
  transfers between devices with their start and end apart: 4 -> 0, of which waited for: 4 -> 0; matrix products, arithmetic and copies ran while one was open for 0% -> 0% of each run, Pallas kernels for 0% -> 0%
where the time goes in v1:
time: 59.4 us; the launch traced here: 59.2 us
  Pallas kernels  55.2 us (93%)
  local copies, waits for them, and re-layouts  3.97 us (7%)
    pallas_call x1, Pallas kernels, per_device(): pl.pallas_call(kernel, out_shape=jax.ShapeDtypeStruct((64, 8, 256), F32),...  55.2 us
    unnamed x7, local copies, waits for them, and re-layouts  3.97 us

profile of v1, /device:TPU:1, one launch (start us, length us, event | category | flops | bytes accessed | tf_op | source)
XLA Modules:
  0.0 59.2 jit_solution(11947752323180563028)
XLA Ops:
  0.0 0.0 copy-start
  0.0 1.5 %copy-done = f32[3,3,3,64,256]{4,3,2,1,0:T(8,128)S(1)} copy-done((f32[3,3,3,64,256]{4,3,2,1,0:T(8,128)S(1)}, f32[3,3,3,64,256]{4,3,2,1,0:T(8,128)}, u32[]{:S(2)}) %copy-start) | copy-done | bytes 1769496
  1.5 0.0 copy-start.1
  1.5 1.0 %copy-done.1 = f32[64,1,8,256]{3,2,1,0:T(8,128)S(1)} copy-done((f32[64,1,8,256]{3,2,1,0:T(8,128)S(1)}, f32[64,1,8,256]{3,2,1,0:T(8,128)}, u32[]{:S(2)}) %copy-start.1) | copy-done | bytes 524312
  2.5 0.0 copy-start.2
  2.5 0.7 %copy-done.2 = f32[64]{0:T(128)S(1)} copy-done((f32[64]{0:T(128)S(1)}, f32[64]{0:T(128)}, u32[]{:S(2)}) %copy-start.2) | copy-done | bytes 280
  3.2 55.2 %convolution.1 = f32[64,8,256]{2,1,0:T(8,128)S(1)} custom-call(f32[64,8,256]{2,1,0:T(8,128)S(1)} %bitcast.7, f32[27,64,256]{2,1,0:T(8,128)S(1)} %bitcast.6, f32[64]{0:T(128)S(1)} %copy-done.2), custom_call_target="tpu_custom_call" | custom-call | flops 4000000000 | bytes 4000000 | tf_op jit(solution)/shard_map/convolution/pallas_call | solution.py:302
  58.4 0.8 %copy.6 = f32[64,1,8,256]{3,2,1,0:T(8,128)} copy(f32[64,1,8,256]{3,2,1,0:T(8,128)S(1)} %bitcast.5) | data formatting | bytes 1048576
Async XLA Ops:
  0.0 1.5 %copy-start = (f32[3,3,3,64,256]{4,3,2,1,0:T(8,128)S(1)}, f32[3,3,3,64,256]{4,3,2,1,0:T(8,128)}, u32[]{:S(2)}) copy-start(f32[3,3,3,64,256]{4,3,2,1,0:T(8,128)} %param.4) | copy-start | bytes 5308420
  1.5 1.0 %copy-start.1 = (f32[64,1,8,256]{3,2,1,0:T(8,128)S(1)}, f32[64,1,8,256]{3,2,1,0:T(8,128)}, u32[]{:S(2)}) copy-start(f32[64,1,8,256]{3,2,1,0:T(8,128)} %param.3) | copy-start | bytes 1572868
  2.5 0.7 %copy-start.2 = (f32[64]{0:T(128)S(1)}, f32[64]{0:T(128)}, u32[]{:S(2)}) copy-start(f32[64]{0:T(128)} %b_ref.1) | copy-start | bytes 772

commit v2 on v0

v2 whole, which is shorter than its diff:
```python
import jax
import jax.numpy as jnp
from jax import lax
from jax.experimental import pallas as pl
from jax.experimental.pallas import tpu as pltpu
from jax.sharding import PartitionSpec as P

MESH = pl.DeviceIdType.MESH
CHUNKS = ((9, 5, 0), (14, 4, 1), (0, 4, 0), (4, 5, 1), (18, 5, 0), (23, 4, 1))
NEAR = (1, 7, 2, 6, 3, 5, 4)
ORDER = (0, 7, 1, 2, 3, 4, 5, 6)
F32, BF16 = jnp.float32, jnp.bfloat16


def split(value):
    high = value.astype(BF16)
    return high, (value - high.astype(F32)).astype(BF16)


def kernel(
    f_ref, w_ref, b_ref, o_ref,
    field, bias, turned, out_in, got_in, cells, taps, weight_own, weight_other, wcat, total, sibling, out_back, got_back, ready,
    own_sem, swap_ss, swap_rs, a_ss, a_rs, b_ss, b_rs, in_ss, in_rs, halo_ss, halo_rs, sib_ss, sib_rs, back_ss, back_rs,
):
    s, c, h = lax.axis_index("space"), lax.axis_index("chan"), lax.axis_index("filt")
    xx, yy = s // 4, s % 4
    lo, core = c // 2, c % 2
    z = 2 * h + lo

    def column(other_z, other_core):
        return (s, (other_z % 2) * 2 + other_core, other_z // 2)

    def plane(other_x, other_y):
        return (other_x * 4 + other_y, c, h)

    def remote(source, target, send, receive, device):
        return pltpu.make_async_remote_copy(
            source, target, send, receive, device_id=device, device_id_type=MESH
        )

    fetch_field = pltpu.make_async_copy(f_ref, field, own_sem.at[0])
    fetch_field.start()

    barrier = pltpu.get_barrier_semaphore()
    greet = []
    for dz in range(8):
        for dk in range(2):
            if dz or dk:
                greet.append(column((z + dz) % 8, (core + dk) % 2))
    for d in range(1, 4):
        greet.append(plane((xx + d) % 4, yy))
        greet.append(plane(xx, (yy + d) % 4))
    greet.append(((s + 1) % 16, c, h))
    greet.append(((s + 15) % 16, c, h))
    for device in greet:
        pl.semaphore_signal(barrier, 1, device_id=device, device_id_type=MESH)
    fetch_weight = pltpu.make_async_copy(w_ref, weight_own, own_sem.at[1])
    fetch_weight.start()
    fetch_bias = pltpu.make_async_copy(b_ref, bias, own_sem.at[2])
    fetch_bias.start()

    lane = lax.broadcasted_iota(jnp.int32, (1, 128), 1)
    left = lane < 64
    fetch_field.wait()
    for x in range(8):
        rows = field[:, x, :]
        turned[x, 8:264, :] = jnp.concatenate([rows, rows], axis=0).T
        turned[x, 0:8, :] = jnp.zeros((8, 128), F32)
        turned[x, 264:272, :] = jnp.zeros((8, 128), F32)
    for t in range(8):
        base = 8 + 32 * t
        low_side = turned[:, base - 8 : base, :][:, 7, :]
        high_side = turned[:, base + 32 : base + 40, :][:, 0, :]
        out_in[t, 0:8, :] = jnp.where(left, low_side, high_side)
        for n, x in enumerate(ORDER):
            out_in[t, 8 + 16 * n : 24 + 16 * n, :] = jnp.where(
                left, turned[x, base : base + 16, :], turned[x, base + 16 : base + 32, :]
            )
    got_in[z] = out_in[z]

    @pl.when(s == 0)
    def _():
        cells[:, 0, :, :] = jnp.zeros((4, 48, 128), F32)

    @pl.when(s == 15)
    def _():
        cells[:, 9, :, :] = jnp.zeros((4, 48, 128), F32)

    pl.semaphore_wait(barrier, len(greet))

    def piece(ref, first, count, turn):
        u, v = (yy, xx) if turn else (xx, yy)
        rows = pl.multiple_of(16 * u + 8 * (v // 2), 8)
        lanes = pl.multiple_of(128 * (v % 2), 128)
        return ref.at[pl.ds(first, count), pl.ds(rows, 8), pl.ds(lanes, 128)]

    def band(ref, first, count, turn):
        u = yy if turn else xx
        return ref.at[pl.ds(first, count), pl.ds(pl.multiple_of(16 * u, 16), 16), :]

    swaps = []
    for q, (first, count, turn) in enumerate(CHUNKS):
        target = column((z + (7 if turn else 1)) % 8, core)
        swaps.append(
            remote(
                piece(w_ref, first, count, turn), piece(weight_other, first, count, turn),
                swap_ss.at[q], swap_rs.at[q], target,
            )
        )
        swaps[-1].start()

    PARTS = (pl.ds(0, 40), pl.ds(40, 96))
    ins = []
    for part in range(2):
        for n, dz in enumerate(NEAR):
            target = (z + dz) % 8
            ins.append(
                remote(
                    out_in.at[target, PARTS[part]], got_in.at[z, PARTS[part]],
                    in_ss.at[part, n], in_rs.at[part, z], column(target, core),
                )
            )
            ins[-1].start()

    def convert(source, half, first, count):
        @pl.loop(first, first + count)
        def _(tap):
            ab, y = tap // 3, tap % 3
            high, low = split(source[tap])
            for place, value in ((256 * y, high), (256 * y + 128, high), (768 + 128 * y, low)):
                wcat[ab, pl.ds(pl.multiple_of(place + 64 * half, 64), 64), :] = value

    fetch_weight.wait()
    convert(weight_own, lo, 0, 13)

    spread_a, spread_b = [], []
    for q, (first, count, turn) in enumerate(CHUNKS):
        swaps[q].wait_recv()
        for d in range(1, 4):
            target = plane((xx + d) % 4, yy) if turn else plane(xx, (yy + d) % 4)
            block = piece(weight_other, first, count, turn)
            copy = remote(block, block, a_ss.at[q, d - 1], a_rs.at[q, d - 1], target)
            copy.start()
            spread_a.append(copy)
    convert(weight_own, lo, 13, 14)
    for q, (first, count, turn) in enumerate(CHUNKS):
        for d in range(3):
            spread_a[3 * q + d].wait_recv()
        for d in range(1, 4):
            target = plane(xx, (yy + d) % 4) if turn else plane((xx + d) % 4, yy)
            block = band(weight_other, first, count, turn)
            copy = remote(block, block, b_ss.at[q, d - 1], b_rs.at[q, d - 1], target)
            copy.start()
            spread_b.append(copy)

    def arrived(part, p):
        for l in range(2):
            source = 2 * p + l

            @pl.when(source != z)
            def _():
                remote(
                    out_in.at[z, PARTS[part]], got_in.at[source, PARTS[part]],
                    in_ss.at[part, 0], in_rs.at[part, source], column(source, core),
                ).wait_recv()

    def unpack(p, n):
        x = ORDER[n]
        first = got_in[2 * p, 8 + 16 * n : 24 + 16 * n, :]
        second = got_in[2 * p + 1, 8 + 16 * n : 24 + 16 * n, :]
        cells[p, 1 + x, 8:24, :] = jnp.where(left, first, pltpu.roll(second, 64, 1))
        cells[p, 1 + x, 24:40, :] = jnp.where(left, pltpu.roll(first, 64, 1), second)

    def spread(p, x):
        for y in range(3):
            high, low = split(cells[p, x, 7 + y : 39 + y, :])
            taps[p, x, :, 256 * y : 256 * y + 128] = high
            taps[p, x, :, 256 * y + 128 : 256 * y + 256] = low
            taps[p, x, :, 768 + 128 * y : 896 + 128 * y] = high

    def boundary(p):
        arrived(0, p)
        first = got_in[2 * p, 0:8, :]
        second = got_in[2 * p + 1, 0:8, :]
        low_side = jnp.where(left, first, pltpu.roll(second, 64, 1))
        high_side = jnp.where(left, pltpu.roll(first, 64, 1), second)
        for x in range(8):
            cells[p, 1 + x, 7:8, :] = low_side[x : x + 1]
            cells[p, 1 + x, 40:41, :] = high_side[x : x + 1]
        unpack(p, 0)
        unpack(p, 1)

    def inside(p):
        arrived(1, p)
        for n in range(2, 8):
            unpack(p, n)

        @pl.loop(1, 9)
        def _(x):
            spread(p, x)

    planes = [(h + d) % 4 for d in (0, 1, 3, 2)]

    @pl.loop(0, 4)
    def _(n):
        boundary((h + n) % 4)

    up = remote(cells.at[:, 8], cells.at[:, 0], halo_ss.at[0], halo_rs.at[0], ((s + 1) % 16, c, h))
    down = remote(cells.at[:, 1], cells.at[:, 9], halo_ss.at[1], halo_rs.at[1], ((s + 15) % 16, c, h))

    @pl.when(s < 15)
    def _():
        up.start()

    @pl.when(s > 0)
    def _():
        down.start()

    for p in planes:
        inside(p)

    @pl.when(s > 0)
    def _():
        up.wait_recv()

    @pl.when(s < 15)
    def _():
        down.wait_recv()

    @pl.loop(0, 4)
    def _(p):
        spread(p, 0)
        spread(p, 9)

    for q, (first, count, turn) in enumerate(CHUNKS):
        for d in range(3):
            spread_b[3 * q + d].wait_recv()
        convert(weight_other, 1 - lo, first, count)

    def left_side(p):
        return jnp.concatenate([taps[p, pl.ds(b, 8)].reshape(256, 1152) for b in range(3)], axis=1)

    def right_side(a):
        return wcat[pl.ds(3 * a, 3)].reshape(3456, 256)

    def convolve(g, inner):
        near, far, onward = 3 * g, 2 - g, 2 - 2 * g
        if inner:
            terms = ((near, 2 - onward), (1 + g, 1), (far, onward))
        else:
            terms = ((near, 1), (1 + g, onward))
        return jnp.dot(
            jnp.concatenate([left_side(p) for p, _ in terms], axis=1),
            jnp.concatenate([right_side(a) for _, a in terms], axis=0),
            preferred_element_type=F32,
        )

    exchanges, backs = [], []
    for inner in range(2):
        total[inner] = convolve(1 - core, inner)
        exchange = remote(
            total.at[inner], sibling.at[inner], sib_ss.at[inner], sib_rs.at[inner], column(z, 1 - core)
        )
        exchange.start()
        exchanges.append(exchange)
        total[2 + inner] = convolve(core, inner)
        exchange.wait_recv()

        p = 1 + core if inner else 3 * core
        for pair in range(2):
            lanes = slice(128 * pair, 128 * pair + 128)
            value = (total[2 + inner, :, lanes] + sibling[inner, :, lanes]).reshape(8, 32, 128)
            low_part = value[:, :16, :].reshape(128, 128)
            high_part = value[:, 16:, :].reshape(128, 128)
            out_back[inner, 2 * pair] = jnp.where(left, low_part, pltpu.roll(high_part, 64, 1))
            out_back[inner, 2 * pair + 1] = jnp.where(left, pltpu.roll(low_part, 64, 1), high_part)
        for d in (2, 1, 3, 0):
            f = (h + d) % 4
            copy = remote(
                out_back.at[inner, f], got_back.at[z], back_ss.at[inner, d], back_rs.at[z], (s, p, f)
            )
            if d == 0:
                here = pltpu.make_async_copy(out_back.at[inner, f], got_back.at[z], back_rs.at[z])

                @pl.when(p == c)
                def _():
                    here.start()

                @pl.when(p != c)
                def _():
                    copy.start()
            else:
                copy.start()
            backs.append((copy, p, d))

    fetch_bias.wait()
    offset = bias[...].reshape(1, 64)
    offset = jnp.concatenate([offset, offset], axis=1)
    for n in range(8):
        source = (z + (0, 1, 7, 2, 6, 3, 5, 4)[n]) % 8
        pltpu.make_async_copy(got_back.at[source], got_back.at[source], back_rs.at[source]).wait()
        value = got_back[source] + offset
        value = value / (1.0 + jnp.exp(-value))
        rows = pl.multiple_of(32 * source, 32)
        ready[:, pl.ds(rows, 16), :] = value.reshape(8, 16, 128)
        ready[:, pl.ds(rows + 16, 16), :] = pltpu.roll(value, 64, 1).reshape(8, 16, 128)
    for x in range(8):
        o_ref[:, x, :] = ready[x].T[:64, :]

    for copy in swaps + spread_a + spread_b + ins + exchanges:
        copy.wait_send()

    @pl.when(s < 15)
    def _():
        up.wait_send()

    @pl.when(s > 0)
    def _():
        down.wait_send()

    for copy, p, d in backs:
        if d == 0:
            @pl.when(p != c)
            def _():
                copy.wait_send()
        else:
            copy.wait_send()


def per_device(field, weight, bias):
    dma, chunks = pltpu.SemaphoreType.DMA, len(CHUNKS)
    result = pl.pallas_call(
        kernel,
        out_shape=jax.ShapeDtypeStruct((64, 8, 256), F32),
        in_specs=[pl.BlockSpec(memory_space=pltpu.HBM)] * 3,
        out_specs=pl.BlockSpec(memory_space=pltpu.VMEM),
        scratch_shapes=[
            pltpu.VMEM((64, 8, 256), F32),
            pltpu.VMEM((64,), F32),
            pltpu.VMEM((8, 272, 128), F32),
            pltpu.VMEM((8, 136, 128), F32),
            pltpu.VMEM((8, 136, 128), F32),
            pltpu.VMEM((4, 10, 48, 128), F32),
            pltpu.VMEM((4, 10, 32, 1152), BF16),
            pltpu.VMEM((27, 64, 256), F32),
            pltpu.VMEM((27, 64, 256), F32),
            pltpu.VMEM((9, 1152, 256), BF16),
            pltpu.VMEM((4, 256, 256), F32),
            pltpu.VMEM((2, 256, 256), F32),
            pltpu.VMEM((2, 4, 128, 128), F32),
            pltpu.VMEM((8, 128, 128), F32),
            pltpu.VMEM((8, 256, 128), F32),
            dma((3,)),
            dma((chunks,)),
            dma((chunks,)),
            dma((chunks, 3)),
            dma((chunks, 3)),
            dma((chunks, 3)),
            dma((chunks, 3)),
            dma((2, 7)),
            dma((2, 8)),
            dma((2,)),
            dma((2,)),
            dma((2,)),
            dma((2,)),
            dma((2, 4)),
            dma((8,)),
        ],
        compiler_params=pltpu.CompilerParams(
            collective_id=0, has_side_effects=True, vmem_limit_bytes=63 * 2**20
        ),
        cost_estimate=pl.CostEstimate(flops=4 * 10**9, bytes_accessed=4 * 10**6, transcendentals=131072),
        name="convolution",
    )(field.reshape(64, 8, 256), weight.reshape(27, 64, 256), bias)
    return result.reshape(64, 1, 8, 256)


def solution(mesh):
    placed = (P("chan", "filt", "space", None), P(None, None, None, "chan", None), P("filt"))
    return jax.shard_map(
        per_device,
        mesh=mesh,
        in_specs=placed,
        out_specs=P("filt", "chan", "space", None),
        check_vma=False,
    )
```

time: 256 us -> 52.6 us (0.21)
  waiting for transfers between devices: 125 us -> 0 us
  matrix products: 55.3 us -> 0 us
  Pallas kernels: 0 us -> 49.8 us
  local copies, waits for them, and re-layouts: 43.8 us -> 1.87 us
  between operations: 13.5 us -> 0.01 us
  other arithmetic: 9.56 us -> 0 us
  starting transfers between devices: 7.78 us -> 0 us
    psum x1 -> x0, waiting for transfers between devices: 66.9 us -> none  [per_device(): summed = lax.psum(running, 'chan')]
    conv_general_dilated x1 -> x0, matrix products: 55.3 us -> none  [convolve(): lax.conv_general_dilated(padded[None], oriented, (1, 1, 1), 'VALID', dime...]
    all_gather x1 -> x0, waiting for transfers between devices: 54.5 us -> none  [per_device(): gathered = lax.all_gather(field, 'filt', axis=1, tiled=True)]
    pallas_call x0 -> x1, Pallas kernels: none -> 49.8 us  [per_device(): pl.pallas_call(kernel, out_shape=jax.ShapeDtypeStruct((64, 8, 256), F32),...]
    unnamed x8 -> x1, local copies, waits for them, and re-layouts: 28.7 us -> 1.87 us
    ppermute x2 -> x0, starting transfers between devices: 7.74 us -> none  [the longest x1 6.45 us: extended(): lax.ppermute(lax.slice_in_dim(block, block.shape[dim] - width, None, axis...]
    broadcast_in_dim x1 -> x0, other arithmetic: 7.51 us -> none  [convolve(): padded[None]]
    broadcast_in_dim x1 -> x0, local copies, waits for them, and re-layouts: 7.12 us -> none  [convolve(): padded[None]]
  transfers between devices with their start and end apart: 4 -> 0, of which waited for: 4 -> 0; matrix products, arithmetic and copies ran while one was open for 0% -> 0% of each run, Pallas kernels for 0% -> 0%
where the time goes in v2:
time: 52.6 us; the launch traced here: 51.7 us
  Pallas kernels  49.8 us (95%)
  local copies, waits for them, and re-layouts  1.87 us (4%)
    pallas_call x1, Pallas kernels, per_device(): pl.pallas_call(kernel, out_shape=jax.ShapeDtypeStruct((64, 8, 256), F32),...  49.8 us
    unnamed x1, local copies, waits for them, and re-layouts  1.87 us

profile of v2, /device:TPU:1, one launch (start us, length us, event | category | flops | bytes accessed | tf_op | source)
XLA Modules:
  0.0 51.7 jit_solution(16012506209550331187)
XLA Ops:
  0.0 49.8 %convolution.1 = f32[64,8,256]{2,1,0:T(8,128)} custom-call(f32[64,8,256]{2,1,0:T(8,128)} %bitcast.7, f32[27,64,256]{2,1,0:T(8,128)} %bitcast.6, f32[64]{0:T(128)} %b_ref.1), custom_call_target="tpu_custom_call" | custom-call | flops 4000000000 | bytes 4000000 | tf_op jit(solution)/shard_map/convolution/pallas_call | solution.py:332
  49.8 1.9 %copy.6 = f32[64,1,8,256]{3,2,1,0:T(8,128)} copy(f32[64,1,8,256]{3,2,1,0:T(8,128)} %bitcast.5) | data formatting | bytes 1048576

commit v3 on v2

v3 whole, which is shorter than its diff:
```python
import jax
import jax.numpy as jnp
from jax import lax
from jax.experimental import pallas as pl
from jax.experimental.pallas import tpu as pltpu
from jax.sharding import PartitionSpec as P

MESH = pl.DeviceIdType.MESH
CHUNKS = ((0, 8, 0), (14, 8, 1), (8, 6, 0), (22, 6, 1))
NEAR = (1, 7, 2, 6, 3, 5, 4)
ORDER = (0, 7, 1, 2, 3, 4, 5, 6)
F32, BF16 = jnp.float32, jnp.bfloat16


def split(value):
    high = value.astype(BF16)
    return high, (value - high.astype(F32)).astype(BF16)


def kernel(
    f_ref, w_ref, b_ref, o_ref,
    field, bias, turned, out_in, got_in, cells, taps, weight_own, weight_other, wcat, total, sibling, out_back, got_back, ready,
    own_sem, swap_ss, swap_rs, a_ss, a_rs, b_ss, b_rs, in_ss, in_rs, halo_ss, halo_rs, sib_ss, sib_rs, back_ss, back_rs,
):
    s, c, h = lax.axis_index("space"), lax.axis_index("chan"), lax.axis_index("filt")
    xx, yy = s // 4, s % 4
    lo, core = c // 2, c % 2
    z = 2 * h + lo

    def column(other_z, other_core):
        return (s, (other_z % 2) * 2 + other_core, other_z // 2)

    def plane(other_x, other_y):
        return (other_x * 4 + other_y, c, h)

    def remote(source, target, send, receive, device):
        return pltpu.make_async_remote_copy(
            source, target, send, receive, device_id=device, device_id_type=MESH
        )

    fetch_field = pltpu.make_async_copy(f_ref, field, own_sem.at[0])
    fetch_field.start()

    barrier = pltpu.get_barrier_semaphore()
    greet = []
    for dz in range(8):
        for dk in range(2):
            if dz or dk:
                greet.append(column((z + dz) % 8, (core + dk) % 2))
    for d in range(1, 4):
        greet.append(plane((xx + d) % 4, yy))
        greet.append(plane(xx, (yy + d) % 4))
    greet.append(((s + 1) % 16, c, h))
    greet.append(((s + 15) % 16, c, h))
    for device in greet:
        pl.semaphore_signal(barrier, 1, device_id=device, device_id_type=MESH)
    fetch_weight = pltpu.make_async_copy(w_ref, weight_own.at[pl.ds(0, 27)], own_sem.at[1])
    fetch_weight.start()
    fetch_bias = pltpu.make_async_copy(b_ref, bias, own_sem.at[2])
    fetch_bias.start()

    lane = lax.broadcasted_iota(jnp.int32, (1, 128), 1)
    left = lane < 64
    fetch_field.wait()
    for x in range(8):
        rows = field[:, x, :]
        turned[x, 8:264, :] = jnp.concatenate([rows, rows], axis=0).T
        turned[x, 0:8, :] = jnp.zeros((8, 128), F32)
        turned[x, 264:272, :] = jnp.zeros((8, 128), F32)
    for t in range(8):
        base = 8 + 32 * t
        low_side = turned[:, base - 8 : base, :][:, 7, :]
        high_side = turned[:, base + 32 : base + 40, :][:, 0, :]
        out_in[t, 0:8, :] = jnp.where(left, low_side, high_side)
        for n, x in enumerate(ORDER):
            out_in[t, 8 + 16 * n : 24 + 16 * n, :] = jnp.where(
                left, turned[x, base : base + 16, :], turned[x, base + 16 : base + 32, :]
            )
    got_in[z] = out_in[z]

    @pl.when(s == 0)
    def _():
        cells[:, 0, :, :] = jnp.zeros((4, 48, 128), F32)

    @pl.when(s == 15)
    def _():
        cells[:, 9, :, :] = jnp.zeros((4, 48, 128), F32)

    pl.semaphore_wait(barrier, len(greet))

    def place(first, count, turn):
        u, v = (yy, xx) if turn else (xx, yy)
        rows = pl.multiple_of(16 * u + 8 * (v // 2), 8)
        return pl.ds(first + (count // 2) * (v % 2), count // 2), pl.ds(rows, 8)

    def piece(m, first, count, turn):
        own_taps, own_rows = place(first, count, turn)
        return weight_other.at[m, own_taps, own_rows, :]

    def band(m, first, count, turn):
        u = yy if turn else xx
        return weight_other.at[m, pl.ds(first, count), pl.ds(pl.multiple_of(16 * u, 16), 16), :]

    swaps = [[], []]

    def swap(m):
        for q, (first, count, turn) in enumerate(CHUNKS):
            target = (z + (7 if turn else 1)) % 8
            own_taps, own_rows = place(first, count, turn)
            lanes = pl.ds(pl.multiple_of(128 * ((target + m) % 2), 128), 128)
            copy = remote(
                weight_own.at[own_taps, own_rows, lanes], piece(m, first, count, turn),
                swap_ss.at[m, q], swap_rs.at[m, q], column(target, core),
            )
            copy.start()
            swaps[m].append(copy)

    weight_own[27] = jnp.zeros((64, 256), F32)
    fetch_weight.wait()
    swap(0)

    PARTS = (pl.ds(0, 40), pl.ds(40, 96))
    ins = []
    for part in range(2):
        for n, dz in enumerate(NEAR):
            target = (z + dz) % 8
            ins.append(
                remote(
                    out_in.at[target, PARTS[part]], got_in.at[z, PARTS[part]],
                    in_ss.at[part, n], in_rs.at[part, z], column(target, core),
                )
            )
            ins[-1].start()
        if part == 0:
            swap(1)

    def convert(m, half, first, count, read):
        @pl.loop(first, first + count)
        def _(tap):
            ab, y = tap // 3, tap % 3
            high, low = split(read(tap))
            for base, value in ((256 * y, high), (256 * y + 128, high), (768 + 128 * y, low)):
                wcat[m, ab, pl.ds(pl.multiple_of(base + 64 * half, 64), 64), :] = value

    for j in range(2):
        convert((j + lo) % 2, lo, 0, 27, lambda tap: weight_own[tap, :, 128 * j : 128 * j + 128])

    spread_a, spread_b = [[], []], [[], []]

    def gather_a(m):
        for q, (first, count, turn) in enumerate(CHUNKS):
            swaps[m][q].wait_recv()
            for d in range(1, 4):
                target = plane((xx + d) % 4, yy) if turn else plane(xx, (yy + d) % 4)
                block = piece(m, first, count, turn)
                copy = remote(block, block, a_ss.at[m, q, d - 1], a_rs.at[m, q, d - 1], target)
                copy.start()
                spread_a[m].append(copy)

    def gather_b(m):
        for q, (first, count, turn) in enumerate(CHUNKS):
            for d in range(3):
                spread_a[m][3 * q + d].wait_recv()
            for d in range(1, 4):
                target = plane(xx, (yy + d) % 4) if turn else plane((xx + d) % 4, yy)
                block = band(m, first, count, turn)
                copy = remote(block, block, b_ss.at[m, q, d - 1], b_rs.at[m, q, d - 1], target)
                copy.start()
                spread_b[m].append(copy)

    def gathered(m):
        for q, (first, count, turn) in enumerate(CHUNKS):
            for d in range(3):
                spread_b[m][3 * q + d].wait_recv()
            convert(m, 1 - lo, first, min(count, 27 - first), lambda tap: weight_other[m, tap])

    gather_a(0)
    gather_b(0)
    gather_a(1)

    def arrived(part, p):
        for l in range(2):
            source = 2 * p + l

            @pl.when(source != z)
            def _():
                remote(
                    out_in.at[z, PARTS[part]], got_in.at[source, PARTS[part]],
                    in_ss.at[part, 0], in_rs.at[part, source], column(source, core),
                ).wait_recv()

    def unpack(p, n):
        x = ORDER[n]
        first = got_in[2 * p, 8 + 16 * n : 24 + 16 * n, :]
        second = got_in[2 * p + 1, 8 + 16 * n : 24 + 16 * n, :]
        cells[p, 1 + x, 8:24, :] = jnp.where(left, first, pltpu.roll(second, 64, 1))
        cells[p, 1 + x, 24:40, :] = jnp.where(left, pltpu.roll(first, 64, 1), second)

    def spread(p, x):
        for y in range(3):
            high, low = split(cells[p, x, 7 + y : 39 + y, :])
            taps[p, x, :, 256 * y : 256 * y + 128] = high
            taps[p, x, :, 256 * y + 128 : 256 * y + 256] = low
            taps[p, x, :, 768 + 128 * y : 896 + 128 * y] = high

    def boundary(p):
        arrived(0, p)
        first = got_in[2 * p, 0:8, :]
        second = got_in[2 * p + 1, 0:8, :]
        low_side = jnp.where(left, first, pltpu.roll(second, 64, 1))
        high_side = jnp.where(left, pltpu.roll(first, 64, 1), second)
        for x in range(8):
            cells[p, 1 + x, 7:8, :] = low_side[x : x + 1]
            cells[p, 1 + x, 40:41, :] = high_side[x : x + 1]
        unpack(p, 0)
        unpack(p, 1)

    def inside(p):
        arrived(1, p)
        for n in range(2, 8):
            unpack(p, n)

        @pl.loop(1, 9)
        def _(x):
            spread(p, x)

    planes = [(h + d) % 4 for d in (0, 1, 3, 2)]

    @pl.loop(0, 4)
    def _(n):
        boundary((h + n) % 4)

    up = remote(cells.at[:, 8], cells.at[:, 0], halo_ss.at[0], halo_rs.at[0], ((s + 1) % 16, c, h))
    down = remote(cells.at[:, 1], cells.at[:, 9], halo_ss.at[1], halo_rs.at[1], ((s + 15) % 16, c, h))

    @pl.when(s < 15)
    def _():
        up.start()

    @pl.when(s > 0)
    def _():
        down.start()

    gather_b(1)
    gathered(0)
    for p in planes:
        inside(p)

    @pl.when(s > 0)
    def _():
        up.wait_recv()

    @pl.when(s < 15)
    def _():
        down.wait_recv()

    @pl.loop(0, 4)
    def _(p):
        spread(p, 0)
        spread(p, 9)

    def left_side(part, p):
        return jnp.concatenate([taps[p, pl.ds(4 * part + b, 4)].reshape(128, 1152) for b in range(3)], axis=1)

    def right_side(m, a):
        return wcat[m, pl.ds(3 * a, 3)].reshape(3456, 128)

    def convolve(target, part, m, g):
        onward = 2 - 2 * g
        middle, ahead = right_side(m, 1), right_side(m, onward)
        target[...] = jnp.dot(
            jnp.concatenate([left_side(part, 3 * g), left_side(part, 1 + g)], axis=1),
            jnp.concatenate(
                [
                    jnp.concatenate([middle, right_side(m, 2 - onward)], axis=1),
                    jnp.concatenate([ahead, middle], axis=1),
                ],
                axis=0,
            ),
            preferred_element_type=F32,
        )
        target[:, 128:] += jnp.dot(left_side(part, 2 - g), ahead, preferred_element_type=F32)

    exchanges, backs = [], []

    def begin(part, m):
        k = 2 * m + part
        convolve(total.at[k, 0], part, m, 1 - core)
        exchange = remote(total.at[k, 0], sibling.at[k], sib_ss.at[k], sib_rs.at[k], column(z, 1 - core))
        exchange.start()
        exchanges.append(exchange)

    def finish(part, m):
        k = 2 * m + part
        convolve(total.at[k, 1], part, m, core)
        exchanges[k].wait_recv()

        for n in range(2):
            p = 1 + core if n else 3 * core
            lanes = slice(128 * n, 128 * n + 128)
            value = (total[k, 1, :, lanes] + sibling[k, :, lanes]).reshape(4, 32, 128)
            low_part = value[:, :16, :].reshape(64, 128)
            high_part = value[:, 16:, :].reshape(64, 128)
            out_back[k, n, 0] = jnp.where(left, low_part, pltpu.roll(high_part, 64, 1))
            out_back[k, n, 1] = jnp.where(left, pltpu.roll(low_part, 64, 1), high_part)
            for j in range(2):
                f = 2 * ((lo + m) % 2) + j
                away = jnp.logical_or(p != c, f != h)
                block, place_back = out_back.at[k, n, j], got_back.at[z, part]
                copy = remote(block, place_back, back_ss.at[k, n, j], back_rs.at[z, part], (s, p, f))
                here = pltpu.make_async_copy(block, place_back, back_rs.at[z, part])
                pl.when(away)(copy.start)
                pl.when(jnp.logical_not(away))(here.start)
                backs.append((copy, away))

    for m in range(2):
        if m:
            gathered(m)
        begin(0, m)
        begin(1, m)
        finish(0, m)
        finish(1, m)

    fetch_bias.wait()
    offset = bias[...].reshape(1, 64)
    offset = jnp.concatenate([offset, offset], axis=1)
    for n in range(16):
        source, part = 2 * (n % 4) + (h // 2 + n // 8) % 2, n // 4 % 2
        arrival = got_back.at[source, part]
        pltpu.make_async_copy(arrival, arrival, back_rs.at[source, part]).wait()
        value = got_back[source, part] + offset
        value = value / (1.0 + jnp.exp(-value))
        rows, columns = pl.multiple_of(32 * source, 32), slice(4 * part, 4 * part + 4)
        ready[columns, pl.ds(rows, 16), :] = value.reshape(4, 16, 128)
        ready[columns, pl.ds(rows + 16, 16), :] = pltpu.roll(value, 64, 1).reshape(4, 16, 128)
    for x in range(8):
        o_ref[:, x, :] = ready[x].T[:64, :]

    for copy in swaps[0] + swaps[1] + spread_a[0] + spread_a[1] + spread_b[0] + spread_b[1] + ins + exchanges:
        copy.wait_send()

    @pl.when(s < 15)
    def _():
        up.wait_send()

    @pl.when(s > 0)
    def _():
        down.wait_send()

    for copy, away in backs:
        pl.when(away)(copy.wait_send)


def per_device(field, weight, bias):
    dma, chunks = pltpu.SemaphoreType.DMA, len(CHUNKS)
    result = pl.pallas_call(
        kernel,
        out_shape=jax.ShapeDtypeStruct((64, 8, 256), F32),
        in_specs=[pl.BlockSpec(memory_space=pltpu.HBM)] * 3,
        out_specs=pl.BlockSpec(memory_space=pltpu.VMEM),
        scratch_shapes=[
            pltpu.VMEM((64, 8, 256), F32),
            pltpu.VMEM((64,), F32),
            pltpu.VMEM((8, 272, 128), F32),
            pltpu.VMEM((8, 136, 128), F32),
            pltpu.VMEM((8, 136, 128), F32),
            pltpu.VMEM((4, 10, 48, 128), F32),
            pltpu.VMEM((4, 10, 32, 1152), BF16),
            pltpu.VMEM((28, 64, 256), F32),
            pltpu.VMEM((2, 28, 64, 128), F32),
            pltpu.VMEM((2, 9, 1152, 128), BF16),
            pltpu.VMEM((4, 2, 128, 256), F32),
            pltpu.VMEM((4, 128, 256), F32),
            pltpu.VMEM((4, 2, 2, 64, 128), F32),
            pltpu.VMEM((8, 2, 64, 128), F32),
            pltpu.VMEM((8, 256, 128), F32),
            dma((3,)),
            dma((2, chunks)),
            dma((2, chunks)),
            dma((2, chunks, 3)),
            dma((2, chunks, 3)),
            dma((2, chunks, 3)),
            dma((2, chunks, 3)),
            dma((2, 7)),
            dma((2, 8)),
            dma((2,)),
            dma((2,)),
            dma((4,)),
            dma((4,)),
            dma((4, 2, 2)),
            dma((8, 2)),
        ],
        compiler_params=pltpu.CompilerParams(
            collective_id=0, has_side_effects=True, vmem_limit_bytes=53 * 2**20
        ),
        cost_estimate=pl.CostEstimate(flops=4 * 10**9, bytes_accessed=4 * 10**6, transcendentals=131072),
        name="convolution",
    )(field.reshape(64, 8, 256), weight.reshape(27, 64, 256), bias)
    return result.reshape(64, 1, 8, 256)


def solution(mesh):
    placed = (P("chan", "filt", "space", None), P(None, None, None, "chan", None), P("filt"))
    return jax.shard_map(
        per_device,
        mesh=mesh,
        in_specs=placed,
        out_specs=P("filt", "chan", "space", None),
        check_vma=False,
    )
```

time: 52.6 us -> 49.5 us (0.941); the launches traced: 51.7 us -> 49.4 us
  Pallas kernels: 49.8 us -> 47.9 us
    pallas_call x1, Pallas kernels: 49.8 us -> 47.9 us  [per_device(): pl.pallas_call(kernel, out_shape=jax.ShapeDtypeStruct((64, 8, 256), F32),...]
    unnamed x1 -> x3, local copies, waits for them, and re-layouts: 1.87 us -> 1.45 us
where the time goes in v3:
time: 49.5 us; the launch traced here: 49.4 us
  Pallas kernels  47.9 us (97%)
  local copies, waits for them, and re-layouts  1.45 us (3%)
    pallas_call x1, Pallas kernels, per_device(): pl.pallas_call(kernel, out_shape=jax.ShapeDtypeStruct((64, 8, 256), F32),...  47.9 us
    unnamed x3, local copies, waits for them, and re-layouts  1.45 us

profile of v3, /device:TPU:1, one launch (start us, length us, event | category | flops | bytes accessed | tf_op | source)
XLA Modules:
  0.0 49.4 jit_solution(9373187738206469132)
XLA Ops:
  0.0 0.0 copy-start
  0.0 0.7 %copy-done = f32[64]{0:T(128)S(1)} copy-done((f32[64]{0:T(128)S(1)}, f32[64]{0:T(128)}, u32[]{:S(2)}) %copy-start) | copy-done | bytes 280
  0.7 47.9 %convolution.1 = f32[64,8,256]{2,1,0:T(8,128)S(1)} custom-call(f32[64,8,256]{2,1,0:T(8,128)} %bitcast.7, f32[27,64,256]{2,1,0:T(8,128)} %bitcast.6, f32[64]{0:T(128)S(1)} %copy-done), custom_call_target="tpu_custom_call" | custom-call | flops 4000000000 | bytes 4000000 | tf_op jit(solution)/shard_map/convolution/pallas_call | solution.py:356
  48.6 0.8 %copy.6 = f32[64,1,8,256]{3,2,1,0:T(8,128)} copy(f32[64,1,8,256]{3,2,1,0:T(8,128)S(1)} %bitcast.5) | data formatting | bytes 1048576
Async XLA Ops:
  0.0 0.7 %copy-start = (f32[64]{0:T(128)S(1)}, f32[64]{0:T(128)}, u32[]{:S(2)}) copy-start(f32[64]{0:T(128)} %b_ref.1) | copy-start | bytes 772

commit v4 on v3

--- a/solution.py
+++ b/solution.py
@@ -18,8 +18,8 @@
 
 
 def kernel(
-    f_ref, w_ref, b_ref, o_ref,
-    field, bias, turned, out_in, got_in, cells, taps, weight_own, weight_other, wcat, total, sibling, out_back, got_back, ready,
+    f_ref, w_ref, o_ref,
+    field, turned, out_in, got_in, cells, taps, weight_own, weight_other, wcat, total, sibling, out_back, got_back, ready,
     own_sem, swap_ss, swap_rs, a_ss, a_rs, b_ss, b_rs, in_ss, in_rs, halo_ss, halo_rs, sib_ss, sib_rs, back_ss, back_rs,
 ):
     s, c, h = lax.axis_index("space"), lax.axis_index("chan"), lax.axis_index("filt")
@@ -38,6 +38,8 @@
             source, target, send, receive, device_id=device, device_id_type=MESH
         )
 
+    fetch_weight = pltpu.make_async_copy(w_ref, weight_own.at[pl.ds(0, 27)], own_sem.at[1])
+    fetch_weight.start()
     fetch_field = pltpu.make_async_copy(f_ref, field, own_sem.at[0])
     fetch_field.start()
 
@@ -54,13 +56,44 @@
     greet.append(((s + 15) % 16, c, h))
     for device in greet:
         pl.semaphore_signal(barrier, 1, device_id=device, device_id_type=MESH)
-    fetch_weight = pltpu.make_async_copy(w_ref, weight_own.at[pl.ds(0, 27)], own_sem.at[1])
-    fetch_weight.start()
-    fetch_bias = pltpu.make_async_copy(b_ref, bias, own_sem.at[2])
-    fetch_bias.start()
 
     lane = lax.broadcasted_iota(jnp.int32, (1, 128), 1)
     left = lane < 64
+
+    weight_own[27] = jnp.zeros((64, 256), F32)
+    fetch_weight.wait()
+    pl.semaphore_wait(barrier, len(greet))
+
+    def place(first, count, turn):
+        u, v = (yy, xx) if turn else (xx, yy)
+        rows = pl.multiple_of(16 * u + 8 * (v // 2), 8)
+        return pl.ds(first + (count // 2) * (v % 2), count // 2), pl.ds(rows, 8)
+
+    def piece(m, first, count, turn):
+        own_taps, own_rows = place(first, count, turn)
+        return weight_other.at[m, own_taps, own_rows, :]
+
+    def band(m, first, count, turn):
+        u = yy if turn else xx
+        return weight_other.at[m, pl.ds(first, count), pl.ds(pl.multiple_of(16 * u, 16), 16), :]
+
+    swaps = [[], []]
+
+    def swap(m):
+        for q, (first, count, turn) in enumerate(CHUNKS):
+            target = (z + (7 if turn else 1)) % 8
+            own_taps, own_rows = place(first, count, turn)
+            lanes = pl.ds(pl.multiple_of(128 * ((target + target // 2 + target // 4 + m) % 2), 128), 128)
+            copy = remote(
+                weight_own.at[own_taps, own_rows, lanes], piece(m, first, count, turn),
+                swap_ss.at[m, q], swap_rs.at[m, q], column(target, core),
+            )
+            copy.start()
+            swaps[m].append(copy)
+
+    swap(0)
+    swap(1)
+
     fetch_field.wait()
     for x in range(8):
         rows = field[:, x, :]
@@ -86,38 +119,6 @@
     def _():
         cells[:, 9, :, :] = jnp.zeros((4, 48, 128), F32)
 
-    pl.semaphore_wait(barrier, len(greet))
-
-    def place(first, count, turn):
-        u, v = (yy, xx) if turn else (xx, yy)
-        rows = pl.multiple_of(16 * u + 8 * (v // 2), 8)
-        return pl.ds(first + (count // 2) * (v % 2), count // 2), pl.ds(rows, 8)
-
-    def piece(m, first, count, turn):
-        own_taps, own_rows = place(first, count, turn)
-        return weight_other.at[m, own_taps, own_rows, :]
-
-    def band(m, first, count, turn):
-        u = yy if turn else xx
-        return weight_other.at[m, pl.ds(first, count), pl.ds(pl.multiple_of(16 * u, 16), 16), :]
-
-    swaps = [[], []]
-
-    def swap(m):
-        for q, (first, count, turn) in enumerate(CHUNKS):
-            target = (z + (7 if turn else 1)) % 8
-            own_taps, own_rows = place(first, count, turn)
-            lanes = pl.ds(pl.multiple_of(128 * ((target + m) % 2), 128), 128)
-            copy = remote(
-                weight_own.at[own_taps, own_rows, lanes], piece(m, first, count, turn),
-                swap_ss.at[m, q], swap_rs.at[m, q], column(target, core),
-            )
-            copy.start()
-            swaps[m].append(copy)
-
-    weight_own[27] = jnp.zeros((64, 256), F32)
-    fetch_weight.wait()
-    swap(0)
 
     PARTS = (pl.ds(0, 40), pl.ds(40, 96))
     ins = []
@@ -131,8 +132,6 @@
                 )
             )
             ins[-1].start()
-        if part == 0:
-            swap(1)
 
     def convert(m, half, first, count, read):
         @pl.loop(first, first + count)
@@ -141,9 +140,6 @@
             high, low = split(read(tap))
             for base, value in ((256 * y, high), (256 * y + 128, high), (768 + 128 * y, low)):
                 wcat[m, ab, pl.ds(pl.multiple_of(base + 64 * half, 64), 64), :] = value
-
-    for j in range(2):
-        convert((j + lo) % 2, lo, 0, 27, lambda tap: weight_own[tap, :, 128 * j : 128 * j + 128])
 
     spread_a, spread_b = [[], []], [[], []]
 
@@ -175,6 +171,8 @@
             convert(m, 1 - lo, first, min(count, 27 - first), lambda tap: weight_other[m, tap])
 
     gather_a(0)
+    for j in range(2):
+        convert((j + lo + h + h // 2) % 2, lo, 0, 27, lambda tap: weight_own[tap, :, 128 * j : 128 * j + 128])
     gather_b(0)
     gather_a(1)
 
@@ -241,8 +239,8 @@
     def _():
         down.start()
 
+    gathered(0)
     gather_b(1)
-    gathered(0)
     for p in planes:
         inside(p)
 
@@ -304,7 +302,7 @@
             out_back[k, n, 0] = jnp.where(left, low_part, pltpu.roll(high_part, 64, 1))
             out_back[k, n, 1] = jnp.where(left, pltpu.roll(low_part, 64, 1), high_part)
             for j in range(2):
-                f = 2 * ((lo + m) % 2) + j
+                f = 2 * ((lo + h + h // 2 + m) % 2) + j
                 away = jnp.logical_or(p != c, f != h)
                 block, place_back = out_back.at[k, n, j], got_back.at[z, part]
                 copy = remote(block, place_back, back_ss.at[k, n, j], back_rs.at[z, part], (s, p, f))
@@ -321,15 +319,11 @@
         finish(0, m)
         finish(1, m)
 
-    fetch_bias.wait()
-    offset = bias[...].reshape(1, 64)
-    offset = jnp.concatenate([offset, offset], axis=1)
     for n in range(16):
-        source, part = 2 * (n % 4) + (h // 2 + n // 8) % 2, n // 4 % 2
+        source, part = 2 * (n % 4) + (h // 2 + n % 4 + n % 4 // 2 + n // 8) % 2, n // 4 % 2
         arrival = got_back.at[source, part]
         pltpu.make_async_copy(arrival, arrival, back_rs.at[source, part]).wait()
-        value = got_back[source, part] + offset
-        value = value / (1.0 + jnp.exp(-value))
+        value = got_back[source, part]
         rows, columns = pl.multiple_of(32 * source, 32), slice(4 * part, 4 * part + 4)
         ready[columns, pl.ds(rows, 16), :] = value.reshape(4, 16, 128)
         ready[columns, pl.ds(rows + 16, 16), :] = pltpu.roll(value, 64, 1).reshape(4, 16, 128)
@@ -356,11 +350,10 @@
     result = pl.pallas_call(
         kernel,
         out_shape=jax.ShapeDtypeStruct((64, 8, 256), F32),
-        in_specs=[pl.BlockSpec(memory_space=pltpu.HBM)] * 3,
+        in_specs=[pl.BlockSpec(memory_space=pltpu.HBM)] * 2,
         out_specs=pl.BlockSpec(memory_space=pltpu.VMEM),
         scratch_shapes=[
             pltpu.VMEM((64, 8, 256), F32),
-            pltpu.VMEM((64,), F32),
             pltpu.VMEM((8, 272, 128), F32),
             pltpu.VMEM((8, 136, 128), F32),
             pltpu.VMEM((8, 136, 128), F32),
@@ -374,7 +367,7 @@
             pltpu.VMEM((4, 2, 2, 64, 128), F32),
             pltpu.VMEM((8, 2, 64, 128), F32),
             pltpu.VMEM((8, 256, 128), F32),
-            dma((3,)),
+            dma((2,)),
             dma((2, chunks)),
             dma((2, chunks)),
             dma((2, chunks, 3)),
@@ -395,8 +388,8 @@
         ),
         cost_estimate=pl.CostEstimate(flops=4 * 10**9, bytes_accessed=4 * 10**6, transcendentals=131072),
         name="convolution",
-    )(field.reshape(64, 8, 256), weight.reshape(27, 64, 256), bias)
-    return result.reshape(64, 1, 8, 256)
+    )(field.reshape(64, 8, 256), weight.reshape(27, 64, 256))
+    return jax.nn.silu(result.reshape(64, 1, 8, 256) + bias[:, None, None, None])
 
 
 def solution(mesh):

time: 49.5 us -> 48.9 us (0.988)
  local copies, waits for them, and re-layouts: 1.45 us -> 0.01 us
  other arithmetic: 0 us -> 1.01 us
    unnamed x3 -> x2, local copies, waits for them, and re-layouts: 1.45 us -> 0.01 us
    mul x0 -> x1, other arithmetic: none -> 1.01 us  [per_device(): jax.nn.silu(result.reshape(64, 1, 8, 256) + bias[:, None, None, None])]
where the time goes in v4:
time: 48.9 us; the launch traced here: 48.8 us
  Pallas kernels  47.8 us (98%)
  other arithmetic  1.01 us (2%)
    pallas_call x1, Pallas kernels, per_device(): pl.pallas_call(kernel, out_shape=jax.ShapeDtypeStruct((64, 8, 256), F32),...  47.8 us
    mul x1, other arithmetic, per_device(): jax.nn.silu(result.reshape(64, 1, 8, 256) + bias[:, None, None, None])  1.01 us

profile of v4, /device:TPU:1, one launch (start us, length us, event | category | flops | bytes accessed | tf_op | source)
XLA Modules:
  0.0 48.8 jit_solution(3164715683416400379)
XLA Ops:
  0.0 0.0 copy-start
  0.0 47.8 %convolution.1 = f32[64,8,256]{2,1,0:T(8,128)S(1)} custom-call(f32[64,8,256]{2,1,0:T(8,128)} %bitcast.7, f32[27,64,256]{2,1,0:T(8,128)} %bitcast.6), custom_call_target="tpu_custom_call" | custom-call | flops 4000000000 | bytes 4000000 | tf_op jit(solution)/shard_map/convolution/pallas_call | solution.py:350
  47.8 0.0 copy-done
  47.8 1.0 %multiply_bitcast_fusion = f32[64,1,8,256]{3,2,1,0:T(8,128)} fusion(f32[64,8,256]{2,1,0:T(8,128)S(1)} %convolution.1, f32[64]{0:T(128)S(1)} %copy-done), kind=kLoop, calls=%fused_computation | loop fusion | flops 655360 | bytes 1048832 | tf_op jit(solution)/shard_map/jit(silu)/mul | solution.py:392
Async XLA Ops:
  0.0 47.8 %copy-start = (f32[64]{0:T(128)S(1)}, f32[64]{0:T(128)}, u32[]{:S(2)}) copy-start(f32[64]{0:T(128)} %param.5) | copy-start | bytes 772

commit v5 on v4

--- a/solution.py
+++ b/solution.py
@@ -244,21 +244,14 @@
     for p in planes:
         inside(p)
 
-    @pl.when(s > 0)
-    def _():
-        up.wait_recv()
-
-    @pl.when(s < 15)
-    def _():
-        down.wait_recv()
-
-    @pl.loop(0, 4)
-    def _(p):
-        spread(p, 0)
-        spread(p, 9)
-
     def left_side(part, p):
-        return jnp.concatenate([taps[p, pl.ds(4 * part + b, 4)].reshape(128, 1152) for b in range(3)], axis=1)
+        def shifted(b):
+            if part == 0:
+                return taps[p, pl.ds(2 + b, 4)].reshape(128, 1152)
+            ends = [taps[p, pl.ds(6 * n + b, 2)].reshape(64, 1152) for n in range(2)]
+            return jnp.concatenate(ends, axis=0)
+
+        return jnp.concatenate([shifted(b) for b in range(3)], axis=1)
 
     def right_side(m, a):
         return wcat[m, pl.ds(3 * a, 3)].reshape(3456, 128)
@@ -315,6 +308,20 @@
         if m:
             gathered(m)
         begin(0, m)
+        if m == 0:
+            @pl.when(s > 0)
+            def _():
+                up.wait_recv()
+
+            @pl.when(s < 15)
+            def _():
+                down.wait_recv()
+
+            @pl.loop(0, 4)
+            def _(p):
+                spread(p, 0)
+                spread(p, 9)
+
         begin(1, m)
         finish(0, m)
         finish(1, m)
@@ -324,9 +331,12 @@
         arrival = got_back.at[source, part]
         pltpu.make_async_copy(arrival, arrival, back_rs.at[source, part]).wait()
         value = got_back[source, part]
-        rows, columns = pl.multiple_of(32 * source, 32), slice(4 * part, 4 * part + 4)
-        ready[columns, pl.ds(rows, 16), :] = value.reshape(4, 16, 128)
-        ready[columns, pl.ds(rows + 16, 16), :] = pltpu.roll(value, 64, 1).reshape(4, 16, 128)
+        rows = pl.multiple_of(32 * source, 32)
+        value, other = value.reshape(4, 16, 128), pltpu.roll(value, 64, 1).reshape(4, 16, 128)
+        for place_x, own_x in (((2, 0),) if part == 0 else ((0, 0), (6, 2))):
+            width = 2 if part else 4
+            ready[place_x : place_x + width, pl.ds(rows, 16), :] = value[own_x : own_x + width]
+            ready[place_x : place_x + width, pl.ds(rows + 16, 16), :] = other[own_x : own_x + width]
     for x in range(8):
         o_ref[:, x, :] = ready[x].T[:64, :]
 

time: 48.9 us -> 48.8 us (level)
  no operation moved by 1% of the time
where the time goes in v5:
time: 48.8 us; the launch traced here: 48.7 us
  Pallas kernels  47.7 us (98%)
  other arithmetic  1.01 us (2%)
    pallas_call x1, Pallas kernels, per_device(): pl.pallas_call(kernel, out_shape=jax.ShapeDtypeStruct((64, 8, 256), F32),...  47.7 us
    mul x1, other arithmetic, per_device(): jax.nn.silu(result.reshape(64, 1, 8, 256) + bias[:, None, None, None])  1.01 us

profile of v5, /device:TPU:1, one launch (start us, length us, event | category | flops | bytes accessed | tf_op | source)
XLA Modules:
  0.0 48.7 jit_solution(1570859128535578598)
XLA Ops:
  0.0 0.0 copy-start
  0.0 47.7 %convolution.1 = f32[64,8,256]{2,1,0:T(8,128)S(1)} custom-call(f32[64,8,256]{2,1,0:T(8,128)} %bitcast.7, f32[27,64,256]{2,1,0:T(8,128)} %bitcast.6), custom_call_target="tpu_custom_call" | custom-call | flops 4000000000 | bytes 4000000 | tf_op jit(solution)/shard_map/convolution/pallas_call | solution.py:360
  47.7 0.0 copy-done
  47.7 1.0 %multiply_bitcast_fusion = f32[64,1,8,256]{3,2,1,0:T(8,128)} fusion(f32[64,8,256]{2,1,0:T(8,128)S(1)} %convolution.1, f32[64]{0:T(128)S(1)} %copy-done), kind=kLoop, calls=%fused_computation | loop fusion | flops 655360 | bytes 1048832 | tf_op jit(solution)/shard_map/jit(silu)/mul | solution.py:402
Async XLA Ops:
  0.0 47.7 %copy-start = (f32[64]{0:T(128)S(1)}, f32[64]{0:T(128)}, u32[]{:S(2)}) copy-start(f32[64]{0:T(128)} %param.5) | copy-start | bytes 772
